TPU v7x, 256 devices: a whole 4x4x8 slice. The times are simulated.
256 devices in a mesh: row: 16 (over y, z_hi, core), col: 16 (over x, z_lo).
Axes of the slice: x: 4, y: 4, z: 8 (z_hi: 2, z_lo: 4; z = z_hi * 4 + z_lo), core: 2. Of those that a mesh axis runs over, the one named last changes fastest.
Arguments:
- inputs: bfloat16 [512, 9216], P(None, 'row'), may hold values from -6 to 6
- target: bfloat16 [512, 9216], P(None, 'row'), may hold values from -6 to 6
- w_in: bfloat16 [9216, 18432], P('row', 'col'), may hold values from -0.0625 to 0.0625
- w_out: bfloat16 [18432, 9216], P('col', 'row'), may hold values from -0.046875 to 0.046875
- probe_in: bfloat16 [9216, 18432], P('row', 'col'), may hold values from -1 to 1, as said below
- probe_out: bfloat16 [18432, 9216], P('col', 'row'), may hold values from -1 to 1, as said below
Outputs:
- hess_in: bfloat16 [9216, 18432], P('row', 'col')
- hess_out: bfloat16 [18432, 9216], P('col', 'row')
Inputs may be any that keep to these rules, and one draw needn't show every extreme that they name: `probe_in`: every entry is +1 or -1. `probe_out`: every entry is +1 or -1.
All inputs are finite; a program needn't handle non-finite values.
Results may differ from a plain program's by a relative error of at most 0.0085.
Values may be sent and summed in bfloat16 or wider, within the bound.
A program may use at most 64 MiB of HBM per device.

v0:
```python
import jax
import jax.numpy as jnp
from jax import lax
from jax.sharding import PartitionSpec as P

D = 9216
FF = 18432


def gelu_parts(pre):
    cdf = 0.5 * (1.0 + lax.erf(pre * 0.7071067811865476))
    dens = jnp.exp(-0.5 * pre * pre) * 0.3989422804014327
    return (pre * cdf, cdf + pre * dens, dens * (2.0 - pre * pre))


def matmul_rows(left, right):
    return lax.dot_general(
        left, right, (((0,), (0,)), ((), ())), preferred_element_type=jnp.float32
    )


def matmul_back(left, right):
    return lax.dot_general(
        left, right, (((1,), (1,)), ((), ())), preferred_element_type=jnp.float32
    )


def on_device(inputs, target, w_in, w_out, probe_in, probe_out):
    scale_in = D ** (-0.5)
    scale_out = FF ** (-0.5)
    loss_scale = inputs.shape[0] ** (-0.5)
    pre = jnp.dot(inputs, w_in, preferred_element_type=jnp.float32)
    pre_t = jnp.dot(inputs, probe_in, preferred_element_type=jnp.float32)
    pre, pre_t = (
        lax.psum_scatter(pre, "row", scatter_dimension=0, tiled=True),
        lax.psum_scatter(pre_t, "row", scatter_dimension=0, tiled=True),
    )
    pre_t = scale_in * pre_t
    value, slope, bend = gelu_parts(pre)
    act_share = value.astype(jnp.bfloat16)
    act_t_share = (slope * pre_t).astype(jnp.bfloat16)
    act, act_t = (
        lax.all_gather(act_share, "row", axis=0, tiled=True),
        lax.all_gather(act_t_share, "row", axis=0, tiled=True),
    )
    out = jnp.dot(act, w_out, preferred_element_type=jnp.float32)
    out_t = jnp.dot(act_t, w_out, preferred_element_type=jnp.float32) + scale_out * jnp.dot(
        act, probe_out, preferred_element_type=jnp.float32
    )
    out, out_t = lax.psum((out, out_t), "col")
    resid = (loss_scale * (out - target.astype(jnp.float32))).astype(jnp.bfloat16)
    resid_t = (loss_scale * out_t).astype(jnp.bfloat16)
    hess_out = matmul_rows(act_t, resid) + matmul_rows(act, resid_t)
    back = matmul_back(resid, w_out)
    back_t = matmul_back(resid_t, w_out) + scale_out * matmul_back(resid, probe_out)
    back, back_t = (
        lax.psum_scatter(back, "row", scatter_dimension=0, tiled=True),
        lax.psum_scatter(back_t, "row", scatter_dimension=0, tiled=True),
    )
    curv_share = (back_t * slope + back * bend * pre_t).astype(jnp.bfloat16)
    curv = lax.all_gather(curv_share, "row", axis=0, tiled=True)
    hess_in = matmul_rows(inputs, curv)
    return (hess_in.astype(jnp.bfloat16), hess_out.astype(jnp.bfloat16))


def solution(mesh):
    placed = (
        P(None, "row"),
        P(None, "row"),
        P("row", "col"),
        P("col", "row"),
        P("row", "col"),
        P("col", "row"),
    )
    return jax.shard_map(
        on_device,
        mesh=mesh,
        in_specs=placed,
        out_specs=(P("row", "col"), P("col", "row")),
        check_vma=False,
    )
```

profile of v0, /device:TPU:1, one launch (start us, length us, event | category | flops | bytes accessed | tf_op | source)
XLA Modules:
  0.0 736.4 jit_solution(411731827221319571)
XLA Ops:
  7.2 4.2 fusion.14
  11.5 1.2 copy-done.7
  12.9 2.6 fusion.15
  15.6 89.2 %reduce-scatter.5.cloned.1.call-done = f32[32,1152]{1,0:T(8,128)} async-done(((f32[512,1152]{1,0:T(8,128)}), f32[32,1152]{1,0:T(8,128)}) %reduce-scatter.5.cloned.1.call-update) | async-done | bytes 147472 | tf_op jit(solution)/shard_map/reduce_scatter | solution.py:35
  104.8 90.4 %reduce-scatter.7.cloned.1.call-done = f32[32,1152]{1,0:T(8,128)} async-done(((f32[512,1152]{1,0:T(8,128)}), f32[32,1152]{1,0:T(8,128)}) %reduce-scatter.7.cloned.1.call-update) | async-done | bytes 147472 | tf_op jit(solution)/shard_map/reduce_scatter | solution.py:36
  195.2 1.7 multiply_convert_fusion.5
  197.0 0.5 all-gather.4.cloned.1.call-update
  197.6 55.3 %all-gather.6.cloned.1.call-done = bf16[512,1152]{1,0:T(8,128)(2,1)} async-done(((bf16[32,1152]{1,0:T(8,128)(2,1)}), bf16[512,1152]{1,0:T(8,128)(2,1)}) %all-gather.6.cloned.1.call-update) | async-done | bytes 1179664 | tf_op jit(solution)/shard_map/all_gather | solution.py:43
  252.9 3.2 fusion.17
  256.1 52.4 %all-gather.4.cloned.1.call-done = bf16[512,1152]{1,0:T(8,128)(2,1)} async-done(((bf16[32,1152]{1,0:T(8,128)(2,1)}), bf16[512,1152]{1,0:T(8,128)(2,1)}) %all-gather.4.cloned.1.call-update) | async-done | bytes 1179664 | tf_op jit(solution)/shard_map/all_gather | solution.py:44
  308.6 2.3 fusion.16
  310.9 2.0 fusion.2
  313.0 164.6 %all-reduce.3.cloned.1.call-done = (f32[512,576]{0,1:T(8,128)}, f32[512,576]{0,1:T(8,128)}) async-done(((f32[512,576]{0,1:T(8,128)}, f32[512,576]{0,1:T(8,128)}), (f32[512,576]{0,1:T(8,128)}, f32[512,576]{0,1:T(8,128)})) %all-reduce.3.cloned.1.call-update) | async-done | bytes 2359312 | tf_op jit(solution)/shard_map/psum | solution.py:50
  477.6 1.5 multiply_convert_fusion
  479.1 2.6 fusion.18
  481.8 2.6 convolution_multiply_fusion
  484.4 2.7 convolution_add_fusion.1
  487.2 91.1 %reduce-scatter.11.cloned.1.call-done = f32[32,1152]{1,0:T(8,128)} async-done(((f32[512,1152]{1,0:T(8,128)}), f32[32,1152]{1,0:T(8,128)}) %reduce-scatter.11.cloned.1.call-update) | async-done | bytes 147472 | tf_op jit(solution)/shard_map/reduce_scatter | solution.py:57
  578.3 90.3 %reduce-scatter.9.cloned.1.call-done = f32[32,1152]{1,0:T(8,128)} async-done(((f32[512,1152]{1,0:T(8,128)}), f32[32,1152]{1,0:T(8,128)}) %reduce-scatter.9.cloned.1.call-update) | async-done | bytes 147472 | tf_op jit(solution)/shard_map/reduce_scatter | solution.py:58
  668.5 1.7 fusion.11
  670.3 2.3 fusion.19
  672.6 2.0 fusion
  674.6 51.7 %all-gather.8.cloned.1.call-done = bf16[512,1152]{1,0:T(8,128)(2,1)} async-done(((bf16[32,1152]{1,0:T(8,128)(2,1)}), bf16[512,1152]{1,0:T(8,128)(2,1)}) %all-gather.8.cloned.1.call-update) | async-done | bytes 1179664 | tf_op jit(solution)/shard_map/all_gather | solution.py:61
  726.3 3.3 fusion.1
  (36 shorter events, 0.6 us)
Async XLA Ops:
  7.2 245.7 %copy-start = (bf16[1152,576]{0,1:T(8,128)(2,1)S(1)}, bf16[1152,576]{0,1:T(8,128)(2,1)}, u32[]{:S(2)}) copy-start(bf16[1152,576]{0,1:T(8,128)(2,1)} %param.9) | copy-start | bytes 3981316
  7.2 97.7 %reduce-scatter.5.cloned.1.call-start = ((), (), s32[]{:S(2)}) async-start(), calls=%async_computation.4 | async-start | bytes 2506752 | tf_op jit(solution)/shard_map/reduce_scatter | solution.py:35
  11.5 1.3 copy-start.7
  11.5 1.5 copy-start.9
  11.5 183.7 %reduce-scatter.7.cloned.1.call-start = ((), (), s32[]{:S(2)}) async-start(), calls=%async_computation.5 | async-start | bytes 2506752 | tf_op jit(solution)/shard_map/reduce_scatter | solution.py:36
  15.6 237.3 %all-gather.6.cloned.1.call-start = ((), (), s32[]{:S(2)}) async-start(), calls=%async_computation.7 | async-start | bytes 1253376 | tf_op jit(solution)/shard_map/all_gather | solution.py:43
  196.9 111.6 %all-gather.4.cloned.1.call-start = ((), (), s32[]{:S(2)}) async-start(), calls=%async_computation.6 | async-start | bytes 1253376 | tf_op jit(solution)/shard_map/all_gather | solution.py:44
  197.5 280.1 %all-reduce.3.cloned.1.call-start = ((), (), s32[]{:S(2)}) async-start(), calls=%async_computation.11 | async-start | bytes 4718592 | tf_op jit(solution)/shard_map/psum | solution.py:50
  256.1 54.8 %copy-start.2 = (bf16[512,1152]{1,0:T(8,128)(2,1)S(1)}, bf16[512,1152]{1,0:T(8,128)(2,1)}, u32[]{:S(2)}) copy-start(bf16[512,1152]{1,0:T(8,128)(2,1)} %all-gather.6.cloned.1.call-done) | copy-start | bytes 3538948
  308.6 2.3 copy-start.8
  312.9 164.7 %copy-start.6 = (bf16[512,576]{0,1:T(8,128)(2,1)S(1)}, bf16[512,576]{0,1:T(8,128)(2,1)}, u32[]{:S(2)}) copy-start(bf16[512,576]{0,1:T(8,128)(2,1)} %param.7) | copy-start | bytes 1769476
  312.9 265.3 %reduce-scatter.11.cloned.1.call-start = ((), (), s32[]{:S(2)}) async-start(), calls=%async_computation.9 | async-start | bytes 2506752 | tf_op jit(solution)/shard_map/reduce_scatter | solution.py:57
  481.7 2.7 copy-start.1
  481.7 186.8 %reduce-scatter.9.cloned.1.call-start = ((), (), s32[]{:S(2)}) async-start(), calls=%async_computation.8 | async-start | bytes 2506752 | tf_op jit(solution)/shard_map/reduce_scatter | solution.py:58
  487.1 181.5 %copy-start.4 = (f32[32,1152]{1,0:T(8,128)S(1)}, f32[32,1152]{1,0:T(8,128)}, u32[]{:S(2)}) copy-start(f32[32,1152]{1,0:T(8,128)} %reduce-scatter.5.cloned.1.call-done) | copy-start | bytes 442372
  487.1 181.5 %copy-start.5 = (f32[32,1152]{1,0:T(8,128)S(1)}, f32[32,1152]{1,0:T(8,128)}, u32[]{:S(2)}) copy-start(f32[32,1152]{1,0:T(8,128)} %reduce-scatter.7.cloned.1.call-done) | copy-start | bytes 442372
  487.1 239.2 %all-gather.8.cloned.1.call-start = ((), (), s32[]{:S(2)}) async-start(), calls=%async_computation.10 | async-start | bytes 1253376 | tf_op jit(solution)/shard_map/all_gather | solution.py:61
  670.3 2.3 copy-start.3
  672.6 53.7 %copy-start.10 = (bf16[512,576]{0,1:T(8,128)(2,1)S(1)}, bf16[512,576]{0,1:T(8,128)(2,1)}, u32[]{:S(2)}) copy-start(bf16[512,576]{0,1:T(8,128)(2,1)} %param.6) | copy-start | bytes 1769476
Sparse Core Ops, SparseCore 0:
  12.3 92.5 reduce-scatter.4
  109.1 86.0 reduce-scatter.6
  198.5 54.3 all-gather.5
  256.0 52.5 all-gather.3
  313.1 164.4 all-reduce.2
  481.9 96.3 reduce-scatter.10
  582.5 85.9 reduce-scatter.8
  671.8 54.4 all-gather.7
where the time goes:
time: 737 us; the launch traced here: 736 us
  waiting for transfers between devices  686 us (93%)
  matrix products  29.9 us (4%)
  between operations  14.2 us (2%)
    psum x1, waiting for transfers between devices, on_device(): out, out_t = lax.psum((out, out_t), 'col')  165 us
    reduce_scatter x1, waiting for transfers between devices, on_device(): lax.psum_scatter(back, 'row', scatter_dimension=0, tiled=True)  91.1 us
    reduce_scatter x1, waiting for transfers between devices, on_device(): lax.psum_scatter(pre_t, 'row', scatter_dimension=0, tiled=True)  90.4 us
    reduce_scatter x1, waiting for transfers between devices, on_device(): lax.psum_scatter(back_t, 'row', scatter_dimension=0, tiled=True)  90.3 us
    reduce_scatter x1, waiting for transfers between devices, on_device(): lax.psum_scatter(pre, 'row', scatter_dimension=0, tiled=True)  89.2 us
    all_gather x1, waiting for transfers between devices, on_device(): lax.all_gather(act_share, 'row', axis=0, tiled=True)  55.3 us
    all_gather x1, waiting for transfers between devices, on_device(): lax.all_gather(act_t_share, 'row', axis=0, tiled=True)  52.4 us
    all_gather x1, waiting for transfers between devices, on_device(): curv = lax.all_gather(curv_share, 'row', axis=0, tiled=True)  51.7 us
  transfers between devices with their start and end apart: 8, of which 8 were waited for; matrix products, arithmetic and copies ran while one was open for 2% of the time, Pallas kernels for 0%

commit v1 on v0

v1 whole, which is shorter than its diff:
```python
import jax
import jax.numpy as jnp
from jax import lax
from jax.experimental import pallas as pl
from jax.experimental.pallas import tpu as pltpu
from jax.sharding import PartitionSpec as P

D = 9216
FF = 18432
MESH = pl.DeviceIdType.MESH
F32 = jnp.float32
BF16 = jnp.bfloat16

PARTS = 4
STAGES = 11

CORE, Y, Z, SHARE_Y, SHARE_CORE = 0, 1, 2, 3, 4
BACK = 5
X, L, SHARE_L, SHARE_X = 10, 11, 12, 13
KINDS = 14


def gelu_parts(pre):
    cdf = 0.5 * (1.0 + lax.erf(pre * 0.7071067811865476))
    dens = jnp.exp(-0.5 * pre * pre) * 0.3989422804014327
    return (pre * cdf, cdf + pre * dens, dens * (2.0 - pre * pre))


def dot(left, right):
    return jnp.dot(left, right, preferred_element_type=F32)


def kernel(
    inputs, target, w_in, w_out, probe_in, probe_out, hess_in, hess_out,
    x_v, tgt_v, w_in_v, w_out_v, p_in_v, p_out_v, w_out_t, p_out_t, x_t,
    ship, got_core, ship_y, got_y, ship_z, got_z, act, slope_v, bend_v, curv,
    ship_x, got_x, ship_l, got_l, resid, load_sem, send_sem, recv_sem,
):
    row, col = lax.axis_index("row"), lax.axis_index("col")
    core, hi, y = lax.rem(row, 2), lax.rem(row // 2, 2), row // 4
    x, low = col // 4, lax.rem(col, 4)
    tokens = x_v.shape[0]
    part = tokens // PARTS
    rows = part // 8
    ff, width = w_out_v.shape
    scale_in, scale_out, loss_scale = D ** (-0.5), FF ** (-0.5), tokens ** (-0.5)

    def at(y_, hi_, core_, x_, low_):
        return {"row": (y_ * 2 + hi_) * 2 + core_, "col": x_ * 4 + low_}

    def turn(i, d):
        return lax.rem(i + d, 4)

    twin = at(y, hi, 1 - core, x, low)
    far = at(y, 1 - hi, core, x, low)
    along_y = [at(turn(y, d), hi, core, x, low) for d in (1, 2, 3)]
    along_x = [at(y, hi, core, turn(x, d), low) for d in (1, 2, 3)]
    along_l = [at(y, hi, core, x, turn(low, d)) for d in (1, 2, 3)]

    loads = [
        pltpu.make_async_copy(src, dst, load_sem.at[k])
        for k, (src, dst) in enumerate(
            [(inputs, x_v), (w_in, w_in_v), (probe_in, p_in_v), (w_out, w_out_v), (probe_out, p_out_v), (target, tgt_v)]
        )
    ]
    for load in loads:
        load.start()

    barrier = pltpu.get_barrier_semaphore()
    peers = [twin, far, *along_y, *along_x, *along_l]
    for peer in peers:
        pl.semaphore_signal(barrier, 1, device_id=peer, device_id_type=MESH)
    pl.semaphore_wait(barrier, len(peers))

    def copies(kind, t, triples):
        return [
            pltpu.make_async_remote_copy(
                src, dst, send_sem.at[kind, t, k], recv_sem.at[kind, t, k], device_id=device, device_id_type=MESH
            )
            for k, (src, dst, device) in enumerate(triples)
        ]

    def core_copies(b, t):
        return copies(CORE + b * BACK, t, [(ship.at[b, t, 1 - core], got_core.at[b, t], twin)])

    def y_copies(b, t):
        return copies(
            Y + b * BACK, t, [(ship_y.at[b, t, turn(y, d)], got_y.at[b, t, d - 1], along_y[d - 1]) for d in (1, 2, 3)]
        )

    def z_copies(b, t):
        return copies(Z + b * BACK, t, [(ship_z.at[b, t], got_z.at[b, t], far)])

    def share_y_copies(b, t):
        held = curv if b else act
        return copies(SHARE_Y + b * BACK, t, [(held.at[t, core, y], held.at[t, core, y], peer) for peer in along_y])

    def share_core_copies(b, t):
        held = curv if b else act
        return copies(SHARE_CORE + b * BACK, t, [(held.at[t, core], held.at[t, core], twin)])

    def x_copies(t):
        return copies(X, t, [(ship_x.at[t, turn(x, d)], got_x.at[t, d - 1], along_x[d - 1]) for d in (1, 2, 3)])

    def l_copies(t):
        return copies(L, t, [(ship_l.at[t, turn(low, d)], got_l.at[t, d - 1], along_l[d - 1]) for d in (1, 2, 3)])

    def share_l_copies(t):
        return copies(SHARE_L, t, [(resid.at[t, x, low], resid.at[t, x, low], peer) for peer in along_l])

    def share_x_copies(t):
        return copies(SHARE_X, t, [(resid.at[t, x], resid.at[t, x], peer) for peer in along_x])

    def start(some):
        for copy in some:
            copy.start()

    def wait(some):
        for copy in some:
            copy.wait()

    def wide(ref):
        return ref[...].astype(F32)

    def put_partials(b, t, first, second):
        shape = (2, 4, rows, ff)
        ship[b, t, :, :, :rows, :] = first.astype(BF16).reshape(shape)
        ship[b, t, :, :, rows:, :] = second.astype(BF16).reshape(shape)
        start(core_copies(b, t))

    def pre_partials(t):
        some = x_v[pl.ds(pl.multiple_of(t * part, part), part), :]
        put_partials(0, t, dot(some, w_in_v[...]), dot(some, p_in_v[...]))

    def sum_cores(b, t):
        wait(core_copies(b, t))
        ship_y[b, t] = (wide(ship.at[b, t, core]) + wide(got_core.at[b, t])).astype(BF16)
        start(y_copies(b, t))

    def sum_y(b, t):
        wait(y_copies(b, t))
        total = wide(ship_y.at[b, t, y])
        for k in range(3):
            total += wide(got_y.at[b, t, k])
        ship_z[b, t] = total.astype(BF16)
        start(z_copies(b, t))

    def sum_z(b, t):
        wait(z_copies(b, t))
        total = wide(ship_z.at[b, t]) + wide(got_z.at[b, t])
        return total[:rows], total[rows:]

    def activate(t):
        pre, pre_t = sum_z(0, t)
        pre_t = scale_in * pre_t
        value, slope, bend = gelu_parts(pre)
        act[t, core, y, :rows, :] = value.astype(BF16)
        act[t, core, y, rows:, :] = (slope * pre_t).astype(BF16)
        start(share_y_copies(0, t))
        slope_v[t] = slope
        bend_v[t] = bend * pre_t

    def pass_on(b, t):
        wait(share_y_copies(b, t))
        start(share_core_copies(b, t))

    def out_partials(t):
        wait(share_core_copies(0, t))
        some = act[t, :, :, :rows, :].reshape(part, ff)
        some_t = act[t, :, :, rows:, :].reshape(part, ff)
        out = dot(some, w_out_v[...])
        out_t = dot(some_t, w_out_v[...]) + scale_out * dot(some, p_out_v[...])
        ship_x[t, 0:2] = out.astype(BF16).reshape(2, part // 2, width)
        ship_x[t, 2:4] = out_t.astype(BF16).reshape(2, part // 2, width)
        start(x_copies(t))

    def sum_x(t):
        wait(x_copies(t))
        total = wide(ship_x.at[t, x])
        for k in range(3):
            total += wide(got_x.at[t, k])
        ship_l[t] = total.astype(BF16).reshape(4, rows, width)
        start(l_copies(t))

    def residuals(t):
        wait(l_copies(t))
        total = wide(ship_l.at[t, low])
        for k in range(3):
            total += wide(got_l.at[t, k])
        first = t * part + lax.rem(x, 2) * (part // 2) + low * rows
        wanted = tgt_v[pl.ds(pl.multiple_of(first, rows), rows), :].astype(F32)
        wanted = wanted * (x < 2).astype(F32)
        resid[t, x, low] = (loss_scale * (total - wanted)).astype(BF16)
        start(share_l_copies(t))

    def pass_on_x(t):
        wait(share_l_copies(t))
        start(share_x_copies(t))

    def back_partials(t):
        wait(share_x_copies(t))
        some = resid[t, 0:2].reshape(part, width)
        some_t = resid[t, 2:4].reshape(part, width)
        back = dot(some, w_out_t[...])
        back_t = dot(some_t, w_out_t[...]) + scale_out * dot(some, p_out_t[...])
        put_partials(1, t, back, back_t)

    def curvature(t):
        back, back_t = sum_z(1, t)
        curv[t, core, y] = (back_t * slope_v[t] + back * bend_v[t]).astype(BF16)
        start(share_y_copies(1, t))

    def second_loads():
        for load in loads[3:]:
            load.wait()

    def transpose():
        for i in range(ff // 128):
            w_out_t[:, i * 128 : (i + 1) * 128] = w_out_v[i * 128 : (i + 1) * 128, :].T
            p_out_t[:, i * 128 : (i + 1) * 128] = p_out_v[i * 128 : (i + 1) * 128, :].T
        for i in range(tokens // 128):
            x_t[:, i * 128 : (i + 1) * 128] = x_v[i * 128 : (i + 1) * 128, :].T

    def outer_out():
        one = resid[:, 0:2].reshape(tokens, width)
        one_t = resid[:, 2:4].reshape(tokens, width)

        @pl.loop(0, ff // 384)
        def _(i):
            cols = pl.ds(pl.multiple_of(i * 384, 384), 384)
            some = act[:, :, :, :rows, cols].reshape(tokens, 384)
            some_t = act[:, :, :, rows:, cols].reshape(tokens, 384)
            hess_out[cols, :] = (dot(some_t.T, one) + dot(some.T, one_t)).astype(BF16)

    steps = [
        (0, lambda t: pre_partials(t)),
        (10, lambda t: pass_on(1, t)),
        (7, lambda t: back_partials(t)),
        (3, lambda t: pass_on(0, t)),
        (9, lambda t: curvature(t)),
        (8, lambda t: sum_y(1, t)),
        (6, lambda t: pass_on_x(t)),
        (5, lambda t: residuals(t)),
        (4, lambda t: sum_x(t)),
        (2, lambda t: activate(t)),
        (1, lambda t: sum_y(0, t)),
        (10, lambda t: wait(share_core_copies(1, t))),
        (7, lambda t: sum_cores(1, t)),
        (3, lambda t: out_partials(t)),
        (0, lambda t: sum_cores(0, t)),
    ]

    for load in loads[:3]:
        load.wait()

    def tick(i, _):
        pl.when(i == 1)(second_loads)
        pl.when(i == 4)(transpose)
        for stage, step in steps:
            t = i - stage

            @pl.when((t >= 0) & (t < PARTS))
            def _(step=step, t=t):
                step(t)

        pl.when(i == STAGES)(outer_out)
        return 0

    lax.fori_loop(0, STAGES + PARTS - 1, tick, 0)

    total = curv[...].reshape(tokens, ff)

    @pl.loop(0, width // 192)
    def _(i):
        cut = pl.ds(pl.multiple_of(i * 192, 192), 192)
        hess_in[cut, :] = dot(x_t[cut, :], total).astype(BF16)


def on_device(inputs, target, w_in, w_out, probe_in, probe_out):
    tokens, width = inputs.shape
    ff = w_in.shape[1]
    part = tokens // PARTS
    rows = part // 8
    two = 2 * rows
    n = PARTS
    return pl.pallas_call(
        kernel,
        out_shape=(jax.ShapeDtypeStruct((width, ff), BF16), jax.ShapeDtypeStruct((ff, width), BF16)),
        in_specs=[pl.BlockSpec(memory_space=pl.ANY)] * 6,
        out_specs=(pl.BlockSpec(memory_space=pltpu.VMEM),) * 2,
        scratch_shapes=[
            pltpu.VMEM((tokens, width), BF16),
            pltpu.VMEM((tokens, width), BF16),
            pltpu.VMEM((width, ff), BF16),
            pltpu.VMEM((ff, width), BF16),
            pltpu.VMEM((width, ff), BF16),
            pltpu.VMEM((ff, width), BF16),
            pltpu.VMEM((width, ff), BF16),
            pltpu.VMEM((width, ff), BF16),
            pltpu.VMEM((width, tokens), BF16),
            pltpu.VMEM((2, n, 2, 4, two, ff), BF16),
            pltpu.VMEM((2, n, 4, two, ff), BF16),
            pltpu.VMEM((2, n, 4, two, ff), BF16),
            pltpu.VMEM((2, n, 3, two, ff), BF16),
            pltpu.VMEM((2, n, two, ff), BF16),
            pltpu.VMEM((2, n, two, ff), BF16),
            pltpu.VMEM((n, 2, 4, two, ff), BF16),
            pltpu.VMEM((n, rows, ff), F32),
            pltpu.VMEM((n, rows, ff), F32),
            pltpu.VMEM((n, 2, 4, rows, ff), BF16),
            pltpu.VMEM((n, 4, part // 2, width), BF16),
            pltpu.VMEM((n, 3, part // 2, width), BF16),
            pltpu.VMEM((n, 4, rows, width), BF16),
            pltpu.VMEM((n, 3, rows, width), BF16),
            pltpu.VMEM((n, 4, 4, rows, width), BF16),
            pltpu.SemaphoreType.DMA((6,)),
            pltpu.SemaphoreType.DMA((KINDS, n, 3)),
            pltpu.SemaphoreType.DMA((KINDS, n, 3)),
        ],
        compiler_params=pltpu.CompilerParams(
            collective_id=0, has_side_effects=True, vmem_limit_bytes=56 * 1024 * 1024
        ),
        cost_estimate=pl.CostEstimate(
            flops=22 * tokens * width * ff, bytes_accessed=12 * width * ff, transcendentals=0
        ),
    )(inputs, target, w_in, w_out, probe_in, probe_out)


def solution(mesh):
    placed = (
        P(None, "row"),
        P(None, "row"),
        P("row", "col"),
        P("col", "row"),
        P("row", "col"),
        P("col", "row"),
    )
    return jax.shard_map(
        on_device,
        mesh=mesh,
        in_specs=placed,
        out_specs=(P("row", "col"), P("col", "row")),
        check_vma=False,
    )
```

time: 737 us -> 118 us (0.16)
  waiting for transfers between devices: 686 us -> 0 us
  Pallas kernels: 0 us -> 106 us
  matrix products: 29.9 us -> 0 us
  between operations: 14.2 us -> 0.66 us
  local copies, waits for them, and re-layouts: 1.43 us -> 11.4 us
    reduce_scatter x4 -> x0, waiting for transfers between devices: 361 us -> none  [the longest x1 91.1 us: on_device(): lax.psum_scatter(back, 'row', scatter_dimension=0, tiled=True)]
    psum x1 -> x0, waiting for transfers between devices: 165 us -> none  [on_device(): out, out_t = lax.psum((out, out_t), 'col')]
    all_gather x3 -> x0, waiting for transfers between devices: 159 us -> none  [the longest x1 55.3 us: on_device(): lax.all_gather(act_share, 'row', axis=0, tiled=True)]
    pallas_call x0 -> x1, Pallas kernels: none -> 106 us  [on_device(): pl.pallas_call(kernel, out_shape=(jax.ShapeDtypeStruct((width, ff), BF16)...]
    dot_general x11 -> x0, matrix products: 29.9 us -> none  [the longest x3 7.91 us: matmul_back(): lax.dot_general(left, right, (((1,), (1,)), ((), ())), preferred_element_...]
  transfers between devices with their start and end apart: 8 -> 0, of which waited for: 8 -> 0; matrix products, arithmetic and copies ran while one was open for 2% -> 0% of each run, Pallas kernels for 0% -> 0%
where the time goes in v1:
time: 118 us
  Pallas kernels  106 us (90%)
  local copies, waits for them, and re-layouts  11.4 us (10%)
    pallas_call x1, Pallas kernels, on_device(): pl.pallas_call(kernel, out_shape=(jax.ShapeDtypeStruct((width, ff), BF16)...  106 us
    unnamed x11, local copies, waits for them, and re-layouts  8.72 us
    pallas_call x1, local copies, waits for them, and re-layouts, on_device(): pl.pallas_call(kernel, out_shape=(jax.ShapeDtypeStruct((width, ff), BF16)...  2.67 us

profile of v1, /device:TPU:1, one launch (start us, length us, event | category | flops | bytes accessed | tf_op | source)
XLA Modules:
  0.0 118.1 jit_solution(13756735565697278808)
XLA Ops:
  0.6 0.0 copy-start.1
  0.6 2.2 %copy.8.inputs = bf16[512,576]{1,0:T(8,128)(2,1)} copy(bf16[512,576]{0,1:T(8,128)(2,1)} %param.6) | data formatting | bytes 1179648 | tf_op args[0]
  2.9 2.1 %copy.9.target = bf16[512,576]{1,0:T(8,128)(2,1)} copy(bf16[512,576]{0,1:T(8,128)(2,1)} %param.7) | data formatting | bytes 1179648 | tf_op args[1]
  5.0 0.0 copy-done.1
  5.0 0.0 copy-start.2
  5.0 1.6 %copy.10.w_out = bf16[1152,576]{1,0:T(8,128)(2,1)} copy(bf16[1152,576]{0,1:T(8,128)(2,1)S(1)} %copy-done.1) | data formatting | bytes 2654208 | tf_op args[3]
  6.7 0.0 copy-done.2
  6.7 1.6 %copy.11.probe_out = bf16[1152,576]{1,0:T(8,128)(2,1)} copy(bf16[1152,576]{0,1:T(8,128)(2,1)S(1)} %copy-done.2) | data formatting | bytes 2654208 | tf_op args[5]
  8.3 106.0 %shard_map.77 = (bf16[576,1152]{1,0:T(8,128)(2,1)}, bf16[1152,576]{1,0:T(8,128)(2,1)}) custom-call(bf16[512,576]{1,0:T(8,128)(2,1)} %copy.8.inputs, bf16[512,576]{1,0:T(8,128)(2,1)} %copy.9.target, bf16[576,1152]{1,0:T(8,128)(2,1)} %w_in.1, bf16[1152,576]{1,0:T(8,128)(2,1)} %copy.10.w_out, bf16[576,1152]{1,0:T(8,128)(2,1)} %probe_in.1, ...), custom_call_target="tpu_custom_call" | custom-call | flops 7474249728 | bytes 7962624 | tf_op jit(solution)/shard_map/pallas_call | solution.py:286
  114.3 0.0 copy-start
  114.3 2.7 %copy.12 = bf16[1152,576]{0,1:T(8,128)(2,1)} copy(bf16[1152,576]{1,0:T(8,128)(2,1)} %get-tuple-element.3) | data formatting | bytes 2654208 | tf_op jit(solution)/shard_map/pallas_call | solution.py:286
  117.0 0.0 copy-done
  117.0 1.1 copy.14
Async XLA Ops:
  0.6 4.4 %copy-start.1 = (bf16[1152,576]{0,1:T(8,128)(2,1)S(1)}, bf16[1152,576]{0,1:T(8,128)(2,1)}, u32[]{:S(2)}) copy-start(bf16[1152,576]{0,1:T(8,128)(2,1)} %param.9) | copy-start | bytes 3981316
  5.0 1.6 %copy-start.2 = (bf16[1152,576]{0,1:T(8,128)(2,1)S(1)}, bf16[1152,576]{0,1:T(8,128)(2,1)}, u32[]{:S(2)}) copy-start(bf16[1152,576]{0,1:T(8,128)(2,1)} %param.11) | copy-start | bytes 3981316
  114.3 2.7 %copy-start = (bf16[576,1152]{1,0:T(8,128)(2,1)S(1)}, bf16[576,1152]{1,0:T(8,128)(2,1)}, u32[]{:S(2)}) copy-start(bf16[576,1152]{1,0:T(8,128)(2,1)} %get-tuple-element.6) | copy-start | bytes 3981316

commit v2 on v1

v2 whole, which is shorter than its diff:
```python
import jax
import jax.numpy as jnp
from jax import lax
from jax.experimental import pallas as pl
from jax.experimental.pallas import tpu as pltpu
from jax.sharding import PartitionSpec as P

D = 9216
FF = 18432
MESH = pl.DeviceIdType.MESH
F32 = jnp.float32
BF16 = jnp.bfloat16

PARTS = 4
GROUP = 128
PERIOD = 3.7

CORE, Y, Z, SHARE_Y, SHARE_CORE = 0, 1, 2, 3, 4
BACK = 5
X, L, SHARE_L, SHARE_X = 10, 11, 12, 13
FIRST = (0, 1, 4, 5, 8, 12, 13, 16, 17, 20, 24, 27, 30, 33)
SEMS = 36


def gelu_parts(pre):
    cdf = 0.5 * (1.0 + lax.erf(pre * 0.7071067811865476))
    dens = jnp.exp(-0.5 * pre * pre) * 0.3989422804014327
    return (pre * cdf, cdf + pre * dens, dens * (2.0 - pre * pre))


def dot(left, right):
    return jnp.dot(left, right, preferred_element_type=F32)


def kernel(
    inputs, target, w_in, w_out, probe_in, probe_out, hess_in, hess_out,
    x_t, tgt_t, tgt_v, w_in_v, p_in_v, w_out_t, p_out_t, w_out_v, p_out_v, resid_t, resid_tt, outer,
    ship, got_core, ship_y, got_y, ship_z, got_z, kept, act, slope_v, bend_v, curv,
    ship_x, got_x, ship_l, got_l, resid, load_sem, send_sem, recv_sem,
):
    row, col = lax.axis_index("row"), lax.axis_index("col")
    core, hi, y = lax.rem(row, 2), lax.rem(row // 2, 2), row // 4
    x, low = col // 4, lax.rem(col, 4)
    tokens = tgt_v.shape[0]
    part = tokens // PARTS
    rows, per = part // 8, GROUP // part
    ff, width = w_out_v.shape
    scale_in, scale_out, loss_scale = D ** (-0.5), FF ** (-0.5), tokens ** (-0.5)

    def at(y_, hi_, core_, x_, low_):
        return {"row": (y_ * 2 + hi_) * 2 + core_, "col": x_ * 4 + low_}

    def turn(i, d):
        return lax.rem(i + d, 4)

    twin = at(y, hi, 1 - core, x, low)
    far = at(y, 1 - hi, core, x, low)
    along_y = [at(turn(y, d), hi, core, x, low) for d in (1, 2, 3)]
    along_x = [at(y, hi, core, turn(x, d), low) for d in (1, 2, 3)]
    along_l = [at(y, hi, core, x, turn(low, d)) for d in (1, 2, 3)]

    loads = [
        pltpu.make_async_copy(src, dst, load_sem.at[k])
        for k, (src, dst) in enumerate(
            [(inputs, x_t), (w_in, w_in_v), (probe_in, p_in_v), (w_out, w_out_t), (probe_out, p_out_t), (target, tgt_t)]
        )
    ]
    for load in loads:
        load.start()

    barrier = pltpu.get_barrier_semaphore()
    peers = [twin, far, *along_y, *along_x, *along_l]
    for peer in peers:
        pl.semaphore_signal(barrier, 1, device_id=peer, device_id_type=MESH)

    def copies(kind, t, triples, first=0):
        return [
            pltpu.make_async_remote_copy(
                src, dst, send_sem.at[t, FIRST[kind] + k], recv_sem.at[t, FIRST[kind] + k], device_id=device, device_id_type=MESH
            )
            for k, (src, dst, device) in enumerate(triples, first)
        ]

    def core_copies(b, t):
        return copies(CORE + b * BACK, t, [(ship.at[b, t, 1 - core], got_core.at[b, t], twin)])

    def y_copies(b, t):
        return copies(
            Y + b * BACK, t, [(ship_y.at[b, t, turn(y, d)], got_y.at[b, t, d - 1], along_y[d - 1]) for d in (1, 2, 3)]
        )

    def z_copies(b, t):
        return copies(Z + b * BACK, t, [(ship_z.at[b, t], got_z.at[b, t], far)])

    def share_y_copies(b, t):
        held = curv if b else act
        return copies(SHARE_Y + b * BACK, t, [(held.at[t, core, y], held.at[t, core, y], peer) for peer in along_y])

    def share_core_copy(b, t, d):
        piece = (curv if b else act).at[t, core, turn(y, 4 - d)]
        return copies(SHARE_CORE + b * BACK, t, [(piece, piece, twin)], d)[0]

    def share_core_copies(b, t):
        return [share_core_copy(b, t, d) for d in (0, 1, 2, 3)]

    def x_copies(t):
        return copies(X, t, [(ship_x.at[t, turn(x, d)], got_x.at[t, d - 1], along_x[d - 1]) for d in (1, 2, 3)])

    def l_copies(t):
        return copies(L, t, [(ship_l.at[t, turn(low, d)], got_l.at[t, d - 1], along_l[d - 1]) for d in (1, 2, 3)])

    def share_l_copies(t):
        return copies(SHARE_L, t, [(resid.at[t, x, low], resid.at[t, x, low], peer) for peer in along_l])

    def share_x_copies(t):
        return copies(SHARE_X, t, [(resid.at[t, x], resid.at[t, x], peer) for peer in along_x])

    def start(some):
        for copy in some[1:2] + some[:1] + some[2:]:
            copy.start()

    def wait(some):
        for copy in some:
            copy.wait()

    def wide(ref):
        return ref[...].astype(F32)

    def flat(value):
        return value.astype(F32).reshape(-1, value.shape[-1]).astype(BF16)

    def put(b, t, which, partial):
        ship[b, t, :, :, which] = partial.reshape(2, 4, rows, ff).astype(BF16)

    def pre_partials(g):
        some = x_t[:, pl.ds(pl.multiple_of(g * GROUP, GROUP), GROUP)].T
        parts = pl.ds(g * per, per)
        ship[0, parts, :, :, 0] = dot(some, w_in_v[...]).reshape(per, 2, 4, rows, ff).astype(BF16)
        ship[0, parts, :, :, 1] = dot(some, p_in_v[...]).reshape(per, 2, 4, rows, ff).astype(BF16)

    def sum_cores(b, t):
        wait(core_copies(b, t))
        ship_y[b, t] = (wide(ship.at[b, t, core]) + wide(got_core.at[b, t])).astype(BF16)
        start(y_copies(b, t))

    def sum_y(b, t):
        wait(y_copies(b, t))
        total = wide(ship.at[b, t, core, y]) + wide(got_core.at[b, t, y])
        for k in range(3):
            total += wide(got_y.at[b, t, k])
        ship_z[b, t] = total.astype(BF16)
        kept[b, t] = total
        start(z_copies(b, t))

    def sum_z(b, t):
        wait(z_copies(b, t))
        total = kept[b, t] + wide(got_z.at[b, t])
        return total[0], total[1]

    def activate(t):
        pre, pre_t = sum_z(0, t)
        pre_t = scale_in * pre_t
        value, slope, bend = gelu_parts(pre)
        act[t, core, y, 0] = value.astype(BF16)
        act[t, core, y, 1] = (slope * pre_t).astype(BF16)
        start(share_y_copies(0, t))
        share_core_copy(0, t, 0).start()
        slope_v[t] = slope
        bend_v[t] = bend * pre_t

    def pass_on(b, t):
        arrive = share_y_copies(b, t)
        for d in (1, 3, 2):
            arrive[d - 1].wait()
            share_core_copy(b, t, d).start()

    def out_partials(t):
        wait(share_core_copies(0, t))
        some, some_t = flat(act[t, :, :, 0]), flat(act[t, :, :, 1])
        out = dot(some, w_out_v[...])
        out_t = dot(some_t, w_out_v[...]) + scale_out * dot(some, p_out_v[...])
        ship_x[t, 0:2] = out.reshape(2, 4, rows, width).astype(BF16)
        ship_x[t, 2:4] = out_t.reshape(2, 4, rows, width).astype(BF16)
        start(x_copies(t))

    def sum_x(t):
        wait(x_copies(t))
        total = wide(ship_x.at[t, x])
        for k in range(3):
            total += wide(got_x.at[t, k])
        ship_l[t] = total.astype(BF16)
        start(l_copies(t))

    def residuals(t):
        wait(l_copies(t))
        total = wide(ship_x.at[t, x, low])
        for k in range(3):
            total += wide(got_x.at[t, k, low])
        for k in range(3):
            total += wide(got_l.at[t, k])
        first = t * part + lax.rem(x, 2) * (part // 2) + low * rows
        wanted = tgt_v[pl.ds(pl.multiple_of(first, rows), rows), :]
        wanted = wanted * (x < 2).astype(F32)
        resid[t, x, low] = (loss_scale * (total - wanted)).astype(BF16)
        start(share_l_copies(t))

    def pass_on_x(t):
        wait(share_l_copies(t))
        start(share_x_copies(t))

    def back_partials(t):
        wait(share_x_copies(t))
        some, some_t = flat(resid[t, 0:2]), flat(resid[t, 2:4])
        back = dot(some, w_out_t[...])
        back_t = dot(some_t, w_out_t[...]) + scale_out * dot(some, p_out_t[...])
        put(1, t, 0, back)
        put(1, t, 1, back_t)
        start(core_copies(1, t))

    def curvature(t):
        back, back_t = sum_z(1, t)
        curv[t, core, y] = (back_t * slope_v[t] + back * bend_v[t]).astype(BF16)
        start(share_y_copies(1, t))
        share_core_copy(1, t, 0).start()

    def turn_w():
        loads[3].wait()
        for i in range(ff // 128):
            w_out_v[i * 128 : (i + 1) * 128, :] = w_out_t[:, i * 128 : (i + 1) * 128].T

    def turn_p():
        loads[4].wait()
        for i in range(ff // 128):
            p_out_v[i * 128 : (i + 1) * 128, :] = p_out_t[:, i * 128 : (i + 1) * 128].T

    def turn_target():
        loads[5].wait()
        for i in range(tokens // 128):
            tgt_v[i * 128 : (i + 1) * 128, :] = tgt_t[:, i * 128 : (i + 1) * 128].T.astype(F32)

    def outer_out():
        resid_t[...] = flat(resid[:, 0:2]).T
        resid_tt[...] = flat(resid[:, 2:4]).T

        @pl.loop(0, ff // 384)
        def _(i):
            cols = pl.ds(pl.multiple_of(i * 384, 384), 384)
            some, some_t = flat(act[:, :, :, 0, :, cols]), flat(act[:, :, :, 1, :, cols])
            hess_out[:, cols] = (dot(resid_t[...], some_t) + dot(resid_tt[...], some)).astype(BF16)

    def outer_in(first, last, add):
        some = flat(curv[first:last])

        @pl.loop(0, width // 192)
        def _(i):
            cut = pl.ds(pl.multiple_of(i * 192, 192), 192)
            product = dot(x_t[cut, first * part : last * part], some)
            if add:
                hess_in[cut, :] = (outer[cut, :] + product).astype(BF16)
            else:
                outer[cut, :] = product

    def next_partials(t):
        if per == 1:
            pre_partials(t)
        else:
            pl.when(lax.rem(t, per) == 0)(lambda: pre_partials(t // per))

    steps = [
        (-1.5, next_partials),
        (0.0, lambda t: start(core_copies(0, t))),
        (5.3, lambda t: sum_cores(0, t)),
        (11.2, lambda t: sum_y(0, t)),
        (19.0, activate),
        (25.7, lambda t: pass_on(0, t)),
        (28.4, out_partials),
        (34.5, sum_x),
        (39.7, residuals),
        (45.3, pass_on_x),
        (52.2, back_partials),
        (54.0, lambda t: sum_cores(1, t)),
        (60.3, lambda t: sum_y(1, t)),
        (71.4, curvature),
        (78.0, lambda t: pass_on(1, t)),
        (83.3, lambda t: wait(share_core_copies(1, t))),
    ]
    order = sorted(((when % PERIOD, int(when // PERIOD), step) for when, step in steps), key=lambda entry: entry[0])
    last_tick = max(stage for _, stage, _ in order)
    back_tick = int(52.2 // PERIOD) + PARTS - 1

    for load in loads[:3]:
        load.wait()
    pre_partials(0)
    pl.semaphore_wait(barrier, len(peers))

    def tick(i, _):
        for _, stage, step in order:
            t = i - stage

            @pl.when((t >= max(0, -stage)) & (t < PARTS))
            def _(step=step, t=t):
                step(t)

        pl.when(i == 0)(turn_w)
        pl.when(i == 1)(turn_p)
        pl.when(i == 2)(turn_target)
        pl.when(i == back_tick)(outer_out)
        pl.when(i == last_tick + PARTS - per - 1)(lambda: outer_in(0, PARTS - per, False))
        return 0

    lax.fori_loop(0, last_tick + PARTS, tick, 0)

    outer_in(PARTS - per, PARTS, True)


def on_device(inputs, target, w_in, w_out, probe_in, probe_out):
    tokens, width = inputs.shape
    ff = w_in.shape[1]
    part = tokens // PARTS
    rows = part // 8
    n = PARTS
    hess_in, hess_out = pl.pallas_call(
        kernel,
        out_shape=(pltpu.VMEM((width, ff), BF16), pltpu.VMEM((width, ff), BF16)),
        in_specs=[pl.BlockSpec(memory_space=pl.ANY)] * 6,
        out_specs=(pl.BlockSpec(memory_space=pltpu.VMEM),) * 2,
        scratch_shapes=[
            pltpu.VMEM((width, tokens), BF16),
            pltpu.VMEM((width, tokens), BF16),
            pltpu.VMEM((tokens, width), F32),
            pltpu.VMEM((width, ff), BF16),
            pltpu.VMEM((width, ff), BF16),
            pltpu.VMEM((width, ff), BF16),
            pltpu.VMEM((width, ff), BF16),
            pltpu.VMEM((ff, width), BF16),
            pltpu.VMEM((ff, width), BF16),
            pltpu.VMEM((width, tokens), BF16),
            pltpu.VMEM((width, tokens), BF16),
            pltpu.VMEM((width, ff), F32),
            pltpu.VMEM((2, n, 2, 4, 2, rows, ff), BF16),
            pltpu.VMEM((2, n, 4, 2, rows, ff), BF16),
            pltpu.VMEM((2, n, 4, 2, rows, ff), BF16),
            pltpu.VMEM((2, n, 3, 2, rows, ff), BF16),
            pltpu.VMEM((2, n, 2, rows, ff), BF16),
            pltpu.VMEM((2, n, 2, rows, ff), BF16),
            pltpu.VMEM((2, n, 2, rows, ff), F32),
            pltpu.VMEM((n, 2, 4, 2, rows, ff), BF16),
            pltpu.VMEM((n, rows, ff), F32),
            pltpu.VMEM((n, rows, ff), F32),
            pltpu.VMEM((n, 2, 4, rows, ff), BF16),
            pltpu.VMEM((n, 4, 4, rows, width), BF16),
            pltpu.VMEM((n, 3, 4, rows, width), BF16),
            pltpu.VMEM((n, 4, rows, width), BF16),
            pltpu.VMEM((n, 3, rows, width), BF16),
            pltpu.VMEM((n, 4, 4, rows, width), BF16),
            pltpu.SemaphoreType.DMA((6,)),
            pltpu.SemaphoreType.DMA((n, SEMS)),
            pltpu.SemaphoreType.DMA((n, SEMS)),
        ],
        compiler_params=pltpu.CompilerParams(
            collective_id=0, has_side_effects=True, vmem_limit_bytes=56 * 1024 * 1024
        ),
        cost_estimate=pl.CostEstimate(
            flops=22 * tokens * width * ff, bytes_accessed=12 * width * ff, transcendentals=0
        ),
    )(inputs.T, target.T, w_in, w_out.T, probe_in, probe_out.T)
    return hess_in, hess_out.T


def solution(mesh):
    placed = (
        P(None, "row"),
        P(None, "row"),
        P("row", "col"),
        P("col", "row"),
        P("row", "col"),
        P("col", "row"),
    )
    return jax.shard_map(
        on_device,
        mesh=mesh,
        in_specs=placed,
        out_specs=(P("row", "col"), P("col", "row")),
        check_vma=False,
    )
```

time: 118 us -> 91.3 us (0.77)
  Pallas kernels: 106 us -> 88.4 us
  local copies, waits for them, and re-layouts: 11.4 us -> 2.13 us
    pallas_call x1, Pallas kernels: 106 us -> 88.4 us  [on_device(): pl.pallas_call(kernel, out_shape=(pltpu.VMEM((width, ff), BF16), pltpu.VM...]
    unnamed x11 -> x2, local copies, waits for them, and re-layouts: 8.72 us -> 2.13 us
    pallas_call x1 -> x0, local copies, waits for them, and re-layouts: 2.67 us -> none  [on_device(): pl.pallas_call(kernel, out_shape=(jax.ShapeDtypeStruct((width, ff), BF16)...]
where the time goes in v2:
time: 91.3 us; the launch traced here: 91.2 us
  Pallas kernels  88.4 us (97%)
  local copies, waits for them, and re-layouts  2.13 us (2%)
    pallas_call x1, Pallas kernels, on_device(): pl.pallas_call(kernel, out_shape=(pltpu.VMEM((width, ff), BF16), pltpu.VM...  88.4 us
    unnamed x2, local copies, waits for them, and re-layouts  2.13 us

profile of v2, /device:TPU:1, one launch (start us, length us, event | category | flops | bytes accessed | tf_op | source)
XLA Modules:
  0.0 91.2 jit_solution(15905225156799667145)
XLA Ops:
  0.6 88.4 %shard_map.77 = (bf16[576,1152]{1,0:T(8,128)(2,1)S(1)}, bf16[576,1152]{1,0:T(8,128)(2,1)S(1)}) custom-call(bf16[576,512]{1,0:T(8,128)(2,1)} %bitcast.8, bf16[576,512]{1,0:T(8,128)(2,1)} %bitcast.9, bf16[576,1152]{1,0:T(8,128)(2,1)} %w_in.1, bf16[576,1152]{1,0:T(8,128)(2,1)} %bitcast.6, bf16[576,1152]{1,0:T(8,128)(2,1)} %probe_in.1, bf16[576,1152]{1,0:T(8,128)(2,1)} %bitcast.7), custom_call_target="tpu_custom_call" | custom-call | flops 7474249728 | bytes 7962624 | tf_op jit(solution)/shard_map/pallas_call | solution.py:322
  89.1 1.1 %copy.10 = bf16[576,1152]{1,0:T(8,128)(2,1)} copy(bf16[576,1152]{1,0:T(8,128)(2,1)S(1)} %get-tuple-element.6) | data formatting | bytes 2654208
  90.2 1.1 %copy.11 = bf16[1152,576]{0,1:T(8,128)(2,1)} copy(bf16[1152,576]{0,1:T(8,128)(2,1)S(1)} %bitcast.5) | data formatting | bytes 2654208

commit v3 on v2

--- a/solution.py
+++ b/solution.py
@@ -119,9 +119,19 @@
         for copy in some[1:2] + some[:1] + some[2:]:
             copy.start()
 
-    def wait(some):
+    def arrived(some):
         for copy in some:
-            copy.wait()
+            copy.wait_recv()
+
+    def sent(some):
+        for copy in some:
+            copy.wait_send()
+
+    def add_arrivals(total, some, refs):
+        for k in (0, 2, 1):
+            some[k].wait_recv()
+            total += wide(refs(k))
+        return total
 
     def wide(ref):
         return ref[...].astype(F32)
@@ -139,21 +149,23 @@
         ship[0, parts, :, :, 1] = dot(some, p_in_v[...]).reshape(per, 2, 4, rows, ff).astype(BF16)
 
     def sum_cores(b, t):
-        wait(core_copies(b, t))
+        before = core_copies(b, t)
+        arrived(before)
         ship_y[b, t] = (wide(ship.at[b, t, core]) + wide(got_core.at[b, t])).astype(BF16)
         start(y_copies(b, t))
+        sent(before)
 
     def sum_y(b, t):
-        wait(y_copies(b, t))
+        before = y_copies(b, t)
         total = wide(ship.at[b, t, core, y]) + wide(got_core.at[b, t, y])
-        for k in range(3):
-            total += wide(got_y.at[b, t, k])
+        total = add_arrivals(total, before, lambda k: got_y.at[b, t, k])
         ship_z[b, t] = total.astype(BF16)
         kept[b, t] = total
         start(z_copies(b, t))
+        sent(before)
 
     def sum_z(b, t):
-        wait(z_copies(b, t))
+        arrived(z_copies(b, t))
         total = kept[b, t] + wide(got_z.at[b, t])
         return total[0], total[1]
 
@@ -165,63 +177,76 @@
         act[t, core, y, 1] = (slope * pre_t).astype(BF16)
         start(share_y_copies(0, t))
         share_core_copy(0, t, 0).start()
+        sent(z_copies(0, t))
         slope_v[t] = slope
         bend_v[t] = bend * pre_t
 
     def pass_on(b, t):
         arrive = share_y_copies(b, t)
         for d in (1, 3, 2):
-            arrive[d - 1].wait()
+            arrive[d - 1].wait_recv()
             share_core_copy(b, t, d).start()
+        sent(arrive)
 
     def out_partials(t):
-        wait(share_core_copies(0, t))
+        before = share_core_copies(0, t)
+        arrived(before)
         some, some_t = flat(act[t, :, :, 0]), flat(act[t, :, :, 1])
         out = dot(some, w_out_v[...])
         out_t = dot(some_t, w_out_v[...]) + scale_out * dot(some, p_out_v[...])
         ship_x[t, 0:2] = out.reshape(2, 4, rows, width).astype(BF16)
         ship_x[t, 2:4] = out_t.reshape(2, 4, rows, width).astype(BF16)
         start(x_copies(t))
+        sent(before)
 
     def sum_x(t):
-        wait(x_copies(t))
-        total = wide(ship_x.at[t, x])
-        for k in range(3):
-            total += wide(got_x.at[t, k])
+        before = x_copies(t)
+        total = add_arrivals(wide(ship_x.at[t, x]), before, lambda k: got_x.at[t, k])
         ship_l[t] = total.astype(BF16)
         start(l_copies(t))
+        sent(before)
 
     def residuals(t):
-        wait(l_copies(t))
+        before = l_copies(t)
         total = wide(ship_x.at[t, x, low])
         for k in range(3):
             total += wide(got_x.at[t, k, low])
-        for k in range(3):
-            total += wide(got_l.at[t, k])
+        total = add_arrivals(total, before, lambda k: got_l.at[t, k])
         first = t * part + lax.rem(x, 2) * (part // 2) + low * rows
         wanted = tgt_v[pl.ds(pl.multiple_of(first, rows), rows), :]
         wanted = wanted * (x < 2).astype(F32)
         resid[t, x, low] = (loss_scale * (total - wanted)).astype(BF16)
         start(share_l_copies(t))
+        sent(before)
 
     def pass_on_x(t):
-        wait(share_l_copies(t))
+        before = share_l_copies(t)
+        arrived(before)
         start(share_x_copies(t))
+        sent(before)
 
     def back_partials(t):
-        wait(share_x_copies(t))
+        before = share_x_copies(t)
+        arrived(before)
         some, some_t = flat(resid[t, 0:2]), flat(resid[t, 2:4])
         back = dot(some, w_out_t[...])
         back_t = dot(some_t, w_out_t[...]) + scale_out * dot(some, p_out_t[...])
         put(1, t, 0, back)
         put(1, t, 1, back_t)
         start(core_copies(1, t))
+        sent(before)
 
     def curvature(t):
         back, back_t = sum_z(1, t)
         curv[t, core, y] = (back_t * slope_v[t] + back * bend_v[t]).astype(BF16)
         start(share_y_copies(1, t))
         share_core_copy(1, t, 0).start()
+        sent(z_copies(1, t))
+
+    def whole_curv(t):
+        before = share_core_copies(1, t)
+        arrived(before)
+        sent(before)
 
     def turn_w():
         loads[3].wait()
@@ -282,7 +307,7 @@
         (60.3, lambda t: sum_y(1, t)),
         (71.4, curvature),
         (78.0, lambda t: pass_on(1, t)),
-        (83.3, lambda t: wait(share_core_copies(1, t))),
+        (83.3, whole_curv),
     ]
     order = sorted(((when % PERIOD, int(when // PERIOD), step) for when, step in steps), key=lambda entry: entry[0])
     last_tick = max(stage for _, stage, _ in order)

time: 91.3 us -> 91.1 us (level)
  no operation moved by 1% of the time
where the time goes in v3:
time: 91.1 us; the launch traced here: 91 us
  Pallas kernels  88.2 us (97%)
  local copies, waits for them, and re-layouts  2.13 us (2%)
    pallas_call x1, Pallas kernels, on_device(): pl.pallas_call(kernel, out_shape=(pltpu.VMEM((width, ff), BF16), pltpu.VM...  88.2 us
    unnamed x2, local copies, waits for them, and re-layouts  2.13 us

profile of v3, /device:TPU:1, one launch (start us, length us, event | category | flops | bytes accessed | tf_op | source)
XLA Modules:
  0.0 91.0 jit_solution(12038435597009511277)
XLA Ops:
  0.6 88.2 %shard_map.77 = (bf16[576,1152]{1,0:T(8,128)(2,1)S(1)}, bf16[576,1152]{1,0:T(8,128)(2,1)S(1)}) custom-call(bf16[576,512]{1,0:T(8,128)(2,1)} %bitcast.8, bf16[576,512]{1,0:T(8,128)(2,1)} %bitcast.9, bf16[576,1152]{1,0:T(8,128)(2,1)} %w_in.1, bf16[576,1152]{1,0:T(8,128)(2,1)} %bitcast.6, bf16[576,1152]{1,0:T(8,128)(2,1)} %probe_in.1, bf16[576,1152]{1,0:T(8,128)(2,1)} %bitcast.7), custom_call_target="tpu_custom_call" | custom-call | flops 7474249728 | bytes 7962624 | tf_op jit(solution)/shard_map/pallas_call | solution.py:347
  88.9 1.1 %copy.10 = bf16[576,1152]{1,0:T(8,128)(2,1)} copy(bf16[576,1152]{1,0:T(8,128)(2,1)S(1)} %get-tuple-element.6) | data formatting | bytes 2654208
  89.9 1.1 %copy.11 = bf16[1152,576]{0,1:T(8,128)(2,1)} copy(bf16[1152,576]{0,1:T(8,128)(2,1)S(1)} %bitcast.5) | data formatting | bytes 2654208

commit v4 on v3

--- a/solution.py
+++ b/solution.py
@@ -326,9 +326,9 @@
             def _(step=step, t=t):
                 step(t)
 
-        pl.when(i == 0)(turn_w)
-        pl.when(i == 1)(turn_p)
-        pl.when(i == 2)(turn_target)
+        pl.when(i == 1)(turn_w)
+        pl.when(i == 2)(turn_p)
+        pl.when(i == 3)(turn_target)
         pl.when(i == back_tick)(outer_out)
         pl.when(i == last_tick + PARTS - per - 1)(lambda: outer_in(0, PARTS - per, False))
         return 0

time: 91.1 us -> 90.4 us (level)
  no operation moved by 1% of the time
where the time goes in v4:
time: 90.4 us; the launch traced here: 90.3 us
  Pallas kernels  87.6 us (97%)
  local copies, waits for them, and re-layouts  2.13 us (2%)
    pallas_call x1, Pallas kernels, on_device(): pl.pallas_call(kernel, out_shape=(pltpu.VMEM((width, ff), BF16), pltpu.VM...  87.6 us
    unnamed x2, local copies, waits for them, and re-layouts  2.13 us

profile of v4, /device:TPU:1, one launch (start us, length us, event | category | flops | bytes accessed | tf_op | source)
XLA Modules:
  0.0 90.3 jit_solution(3899123263173081167)
XLA Ops:
  0.6 87.6 %shard_map.77 = (bf16[576,1152]{1,0:T(8,128)(2,1)S(1)}, bf16[576,1152]{1,0:T(8,128)(2,1)S(1)}) custom-call(bf16[576,512]{1,0:T(8,128)(2,1)} %bitcast.8, bf16[576,512]{1,0:T(8,128)(2,1)} %bitcast.9, bf16[576,1152]{1,0:T(8,128)(2,1)} %w_in.1, bf16[576,1152]{1,0:T(8,128)(2,1)} %bitcast.6, bf16[576,1152]{1,0:T(8,128)(2,1)} %probe_in.1, bf16[576,1152]{1,0:T(8,128)(2,1)} %bitcast.7), custom_call_target="tpu_custom_call" | custom-call | flops 7474249728 | bytes 7962624 | tf_op jit(solution)/shard_map/pallas_call | solution.py:347
  88.2 1.1 %copy.10 = bf16[576,1152]{1,0:T(8,128)(2,1)} copy(bf16[576,1152]{1,0:T(8,128)(2,1)S(1)} %get-tuple-element.6) | data formatting | bytes 2654208
  89.3 1.1 %copy.11 = bf16[1152,576]{0,1:T(8,128)(2,1)} copy(bf16[1152,576]{0,1:T(8,128)(2,1)S(1)} %bitcast.5) | data formatting | bytes 2654208
